TPU v7x, 32 devices: a whole 2x2x4 slice. The times are simulated.
32 devices in a mesh: groups: 1, slab: 32 (over z, y, x, core).
Axes of the slice: x: 2, y: 2, z: 4, core: 2. Of those that a mesh axis runs over, the one named last changes fastest.
Arguments:
- eigvecs: bfloat16 [32, 2, 3, 128, 512], P(('groups', 'slab')), may hold values from -6 to 6
- links: bfloat16 [32, 3, 2, 3, 3, 512], P(('groups', 'slab')), may hold values from -4 to 4
- momenta: int32 [4, 3], replicated, may hold values from -2 to 2
- directions: int32 [4], replicated, may hold values from 0 to 5, as said below
- pairs: int32 [32, 2], P(('groups', 'slab')), may hold values from 0 to 1
- perambulators: bfloat16 [32, 2, 512, 512], P(('groups', 'slab')), may hold values from -0.25 to 0.25
Outputs:
- elementals: float32 [2048, 128], P(('groups', 'slab'))
- correlators: float32 [32, 4, 2], P(('groups', 'slab'))
Inputs may be any that keep to these rules, and one draw needn't show every extreme that they name: `directions`: code 2 a + d is one link step along axis a (0 x, 1 y, 2 z), forward if d = 0 and backward if d = 1; codes 4 and 5 both occur.
All inputs are finite; a program needn't handle non-finite values.
Results may differ from a plain program's by a relative error of at most 0.0057.
Values may be sent and summed in bfloat16 or wider, within the bound.
A program may use at most 128 MiB of HBM per device.

v0:
```python
import functools
import math

import jax
import jax.numpy as jnp
from jax import lax
from jax.experimental import pallas as pl
from jax.experimental.pallas import tpu as pltpu
from jax.sharding import PartitionSpec as P

SPIN = 4
MOM = 4
LX = 16
LY = 16
LZ = 32
ZBLK = 16
MESH = pl.DeviceIdType.MESH
VMEM_LIMIT = 48 * 1024 * 1024


def elementals_kernel(scale, codes, vecs, above, gauge, out, held, wave):
    count, sites = vecs.shape[2], vecs.shape[3]
    plane = above.shape[3]
    lane = lax.broadcasted_iota(jnp.int32, (count, sites), 1)
    ends = {0: lane % LX == LX - 1, 1: (lane // LX) % LY == LY - 1}

    for axis, (near, span) in {0: (1, LX), 1: (LX, plane)}.items():
        used = functools.reduce(jnp.logical_or, [codes[m] // 2 == axis for m in range(MOM)])

        @pl.when(used)
        def _(axis=axis, near=near, span=span):
            for part in range(2):
                for c in range(3):
                    field = vecs[part, c].astype(jnp.float32)
                    inner = pltpu.roll(field, sites - near, 1)
                    outer = pltpu.roll(field, span - near, 1)
                    moved = jnp.where(ends[axis], outer, inner)
                    held[axis, c, pl.ds(part * count, count), :] = moved.astype(jnp.bfloat16)

    for part in range(2):
        for c in range(3):
            rows = pl.ds(part * count, count)
            held[3, c, rows, :] = vecs[part, c]
            held[2, c, rows, pl.ds(0, sites - plane)] = vecs[part, c, :, pl.ds(plane, sites - plane)]
            held[2, c, rows, pl.ds(sites - plane, plane)] = above[part, c]

    for m in range(MOM):
        code = codes[m]
        axis = code // 2
        forward = code % 2 == 0
        source = jnp.where(forward, axis, 3)
        left = jnp.where(forward, 3, axis)
        for start in range(0, sites, 128):
            lanes = pl.ds(start, 128)
            links = [gauge[m, pl.ds(k, 1), lanes] for k in range(18)]

            def rows_step(r, carry, lanes=lanes, links=links):
                row = pl.multiple_of(r * 16, 16)
                fields = [
                    [
                        held[source, b, pl.ds(part * count + row, 16), lanes].astype(jnp.float32)
                        for part in range(2)
                    ]
                    for b in range(3)
                ]
                for c in range(3):
                    real = None
                    imag = None
                    for b in range(3):
                        gr, gi = links[(c * 3 + b) * 2], links[(c * 3 + b) * 2 + 1]
                        xr, xi = fields[b]
                        tr = gr * xr - gi * xi
                        ti = gr * xi + gi * xr
                        real = tr if real is None else real + tr
                        imag = ti if imag is None else imag + ti
                    wave[c, pl.ds(row, 16), lanes] = real.astype(jnp.bfloat16)
                    wave[c, pl.ds(count + row, 16), lanes] = imag.astype(jnp.bfloat16)
                return carry

            lax.fori_loop(0, count // 16, rows_step, 0, unroll=True)
        total = jnp.zeros((2 * count, 2 * count), jnp.float32)
        for c in range(3):
            total = total + lax.dot_general(
                held[left, c],
                wave[c],
                (((1,), (1,)), ((), ())),
                preferred_element_type=jnp.float32,
            )
        real = total[:count, :count] + total[count:, count:]
        imag = total[:count, count:] - total[count:, :count]
        out[m, 0] = (real * scale).astype(jnp.bfloat16)
        out[m, 1] = (imag * scale).astype(jnp.bfloat16)


def exchange_kernel(slab, part, mine, table, landed, held, send, arrive, send_far, send_near, got):
    rows = mine.shape[0]
    groups = slab // ZBLK
    me = lax.axis_index("slab")
    zblock, time = me // groups, me % groups
    own_time = me // ZBLK
    chips = slab // 2
    chip, core = me // 2, me % 2
    partner = chip * 2 + (1 - core)

    barrier = pltpu.get_barrier_semaphore()

    def greet(j, carry):
        pl.semaphore_signal(
            barrier, inc=1, device_id={"slab": lax.rem(me + j, slab)}, device_id_type=MESH
        )
        return carry

    lax.fori_loop(1, slab, greet, 0)
    pl.semaphore_wait(barrier, slab - 1)

    def piece(k):
        return pltpu.make_async_remote_copy(
            src_ref=part.at[pl.ds(pl.multiple_of(k * rows, rows), rows)],
            dst_ref=landed.at[zblock],
            send_sem=send.at[k],
            recv_sem=arrive.at[zblock],
            device_id={"slab": time * ZBLK + k},
            device_id_type=MESH,
        )

    def coming(z):
        return pltpu.make_async_remote_copy(
            src_ref=part.at[pl.ds(0, rows)],
            dst_ref=landed.at[z],
            send_sem=send.at[0],
            recv_sem=arrive.at[z],
            device_id={"slab": partner},
            device_id_type=MESH,
        )

    def send_piece(j, carry):
        k = lax.rem(zblock + j, ZBLK)

        @pl.when(time * ZBLK + k != me)
        def _():
            piece(k).start()

        @pl.when(time * ZBLK + k == me)
        def _():
            landed[zblock] = part[pl.ds(pl.multiple_of(k * rows, rows), rows)]

        return carry

    lax.fori_loop(0, ZBLK, send_piece, 0)

    def take_piece(z, total):
        @pl.when(z * groups + own_time != me)
        def _():
            coming(z).wait_recv()

        return total + landed[z].astype(jnp.float32)

    total = lax.fori_loop(0, ZBLK, take_piece, jnp.zeros(mine.shape, jnp.float32))
    mine[...] = total
    held[me] = total.astype(jnp.bfloat16)

    def block(slot, target, sem):
        return pltpu.make_async_remote_copy(
            src_ref=held.at[slot],
            dst_ref=held.at[slot],
            send_sem=sem,
            recv_sem=got.at[slot],
            device_id={"slab": target},
            device_id_type=MESH,
        )

    block(me, partner, send_near.at[chip]).start()

    def send_far_block(j, carry):
        target = lax.rem(chip + j, chips)
        block(me, target * 2 + core, send_far.at[target]).start()
        return carry

    lax.fori_loop(1, chips, send_far_block, 0)

    def forward(j, carry):
        origin = lax.rem(chip + chips - j, chips)
        slot = origin * 2 + core
        block(slot, partner, send_near.at[origin]).wait_recv()
        block(slot, partner, send_near.at[origin]).start()
        return carry

    lax.fori_loop(1, chips, forward, 0)

    def finish(c, carry):
        block(c * 2 + 1 - core, partner, send_near.at[c]).wait_recv()
        block(c * 2 + core, partner, send_near.at[c]).wait_send()

        @pl.when(c != chip)
        def _():
            block(me, c * 2 + core, send_far.at[c]).wait_send()

        return carry

    lax.fori_loop(0, chips, finish, 0)

    def sent(k, carry):
        @pl.when(time * ZBLK + k != me)
        def _():
            piece(k).wait_send()

        return carry

    lax.fori_loop(0, ZBLK, sent, 0)
    table[...] = held[...]


def correlate_kernel(pairs, phi, tau, out):
    n = pl.program_id(0)
    first, second = pairs[n, 0], pairs[n, 1]
    count = phi.shape[-1]
    size = SPIN * count
    for m in range(MOM):
        fr, fi = phi[first, m, 0], phi[first, m, 1]
        sr, si = phi[second, m, 0], phi[second, m, 1]
        sink = jnp.concatenate(
            [jnp.concatenate([fr, -fi], axis=1), jnp.concatenate([fi, fr], axis=1)], axis=0
        )
        source = jnp.concatenate(
            [jnp.concatenate([sr, si], axis=1), jnp.concatenate([-si, sr], axis=1)], axis=0
        )
        real = jnp.zeros((count, count), jnp.float32)
        imag = jnp.zeros((count, count), jnp.float32)
        for a in range(SPIN):
            rows = slice(a * count, (a + 1) * count)
            stacked = jnp.concatenate([tau[0, 0, rows], tau[0, 1, rows]], axis=0)
            moved = jnp.dot(sink, stacked, preferred_element_type=jnp.float32)
            for b in range(SPIN):
                cols = slice(b * count, (b + 1) * count)
                beside = jnp.concatenate([tau[0, 0, rows, cols], tau[0, 1, rows, cols]], axis=1)
                cross = jnp.dot(beside, source, preferred_element_type=jnp.float32)
                mr, mi = moved[:count, cols], moved[count:, cols]
                cr, ci = cross[:, :count], cross[:, count:]
                tr = mr * cr + mi * ci
                ti = mi * cr - mr * ci
                if (a < 2) == (b < 2):
                    real, imag = real + tr, imag + ti
                else:
                    real, imag = real - tr, imag - ti
        out[n, m, 0] = jnp.sum(real) / size
        out[n, m, 1] = jnp.sum(imag) / size


def phased_links(links, momenta, directions, zblock, depth):
    site_count = links.shape[-1]
    local = jnp.arange(site_count, dtype=jnp.int32)
    axis = directions // 2
    back = directions % 2
    xpos = (local % LX)[None, :] + (back * (axis == 0))[:, None]
    ypos = (local // LX % LY)[None, :] + (back * (axis == 1))[:, None]
    zpos = (local // (LX * LY) + zblock * depth)[None, :] + (back * (axis == 2))[:, None]
    frac = jnp.mod(momenta[:, 0:1] * xpos, LX).astype(jnp.float32) / LX
    frac = frac + jnp.mod(momenta[:, 1:2] * ypos, LY).astype(jnp.float32) / LY
    frac = frac + jnp.mod(momenta[:, 2:3] * zpos, LZ).astype(jnp.float32) / LZ
    angle = 2.0 * math.pi * frac
    cosine, sine = jnp.cos(angle)[:, None, None], jnp.sin(angle)[:, None, None]
    field = links.astype(jnp.float32)
    a = axis[:, None, None, None]
    chosen = [
        jnp.where(a == 0, field[0, p], jnp.where(a == 1, field[1, p], field[2, p]))
        for p in range(2)
    ]
    adjoint = (back == 1)[:, None, None, None]
    real = jnp.where(adjoint, jnp.swapaxes(chosen[0], 1, 2), chosen[0])
    imag = jnp.where(adjoint, -jnp.swapaxes(chosen[1], 1, 2), chosen[1])
    both = jnp.stack([real * cosine + imag * sine, imag * cosine - real * sine], axis=3)
    return both.reshape(directions.shape[0], 18, site_count)


def on_device(eigvecs, links, momenta, directions, pairs, perambulators):
    count = eigvecs.shape[3]
    site_count = eigvecs.shape[4]
    slab = lax.axis_size("slab")
    groups = slab // ZBLK
    plane = LX * LY
    position = lax.axis_index("slab")
    route = [((i + groups) % slab, i) for i in range(slab)]
    above = lax.ppermute(eigvecs[0, ..., :plane], "slab", route)
    gauge = phased_links(links[0], momenta, directions, position // groups, site_count // plane)
    scale = 1.0 / math.sqrt(3.0 * site_count * ZBLK)
    vmem = pl.BlockSpec(memory_space=pltpu.VMEM)
    smem = pl.BlockSpec(memory_space=pltpu.SMEM)
    part = pl.pallas_call(
        functools.partial(elementals_kernel, scale),
        out_shape=jax.ShapeDtypeStruct((MOM, 2, count, count), jnp.bfloat16),
        in_specs=[smem, vmem, vmem, vmem],
        out_specs=vmem,
        scratch_shapes=[
            pltpu.VMEM((4, 3, 2 * count, site_count), jnp.bfloat16),
            pltpu.VMEM((3, 2 * count, site_count), jnp.bfloat16),
        ],
        compiler_params=pltpu.CompilerParams(vmem_limit_bytes=VMEM_LIMIT),
        name="elementals",
    )(directions, eigvecs[0], above, gauge)
    part = part.reshape(MOM * 2 * count, count)
    share = part.shape[0] // ZBLK
    mine, table = pl.pallas_call(
        functools.partial(exchange_kernel, slab),
        out_shape=(
            jax.ShapeDtypeStruct((share, count), jnp.float32),
            jax.ShapeDtypeStruct((slab, share, count), jnp.bfloat16),
        ),
        in_specs=[vmem],
        out_specs=(vmem, vmem),
        scratch_shapes=[
            pltpu.VMEM((ZBLK, share, count), jnp.bfloat16),
            pltpu.VMEM((slab, share, count), jnp.bfloat16),
            pltpu.SemaphoreType.DMA((ZBLK,)),
            pltpu.SemaphoreType.DMA((ZBLK,)),
            pltpu.SemaphoreType.DMA((slab // 2,)),
            pltpu.SemaphoreType.DMA((slab // 2,)),
            pltpu.SemaphoreType.DMA((slab,)),
        ],
        compiler_params=pltpu.CompilerParams(
            collective_id=0, has_side_effects=True, vmem_limit_bytes=VMEM_LIMIT
        ),
        name="exchange",
    )(part)
    phi = table.reshape(groups, MOM, 2, count, count)
    correlators = pl.pallas_call(
        correlate_kernel,
        grid=(pairs.shape[0],),
        out_shape=jax.ShapeDtypeStruct((pairs.shape[0], MOM, 2), jnp.float32),
        in_specs=[
            smem,
            vmem,
            pl.BlockSpec((1,) + perambulators.shape[1:], lambda n: (n, 0, 0, 0)),
        ],
        out_specs=smem,
        compiler_params=pltpu.CompilerParams(vmem_limit_bytes=VMEM_LIMIT),
        name="correlate",
    )(pairs, phi, perambulators)
    return (mine, correlators)


def solution(mesh):
    return jax.shard_map(
        on_device,
        mesh=mesh,
        in_specs=(
            P(("groups", "slab"), None, None, None, None),
            P(("groups", "slab"), None, None, None, None, None),
            P(),
            P(),
            P(("groups", "slab"), None),
            P(("groups", "slab"), None, None, None),
        ),
        out_specs=(P(("groups", "slab"), None), P(("groups", "slab"), None, None)),
        check_vma=False,
    )
```

profile of v0, /device:TPU:0, one launch (start us, length us, event | category | flops | bytes accessed | tf_op | source)
XLA Modules:
  0.0 50.0 jit_solution(15976624991440629402)
XLA Ops:
  0.6 0.0 copy-start.4
  0.6 1.0 %slice_bitcast_fusion = bf16[2,3,128,256]{3,2,1,0:T(8,128)(2,1)S(1)} fusion(bf16[1,2,3,128,512]{4,3,2,1,0:T(8,128)(2,1)} %param.6), kind=kLoop, calls=%fused_computation | loop fusion | bytes 786432 | tf_op jit(solution)/shard_map/squeeze | solution.py:283
  1.7 7.0 %collective-permute-start = (bf16[2,3,128,256]{3,2,1,0:T(8,128)(2,1)S(1)}, bf16[2,3,128,256]{3,2,1,0:T(8,128)(2,1)S(1)}, u32[]{:S(2)}, u32[]{:S(2)}) collective-permute-start(bf16[2,3,128,256]{3,2,1,0:T(8,128)(2,1)S(1)} %slice_bitcast_fusion), channel_id=1, source_target_pairs={{2,0},{3,1},{4,2},{5,3},{6,4},{7,5},{8,6},{9,7},{10,8},{11,9},{12,... | collective-permute-start | bytes 1179656 | tf_op jit(solution)/shard_map/ppermute | solution.py:283
  8.7 0.0 copy-done.4
  8.7 0.1 fusion.21
  8.8 0.0 copy-start.2
  8.8 0.0 copy-start.5
  8.9 0.0 copy-start
  9.0 0.5 %copy-done.2 = s32[4]{0:T(128)S(1)} copy-done((s32[4]{0:T(128)S(1)}, s32[4]{0:T(128)}, u32[]{:S(2)}) %copy-start.2) | copy-done | bytes 40
  9.5 0.0 copy-done.5
  9.5 0.2 slice_reduce_fusion.2
  9.7 0.2 fusion.20
  9.9 0.2 multiply_add_fusion
  10.2 0.0 copy-start.1
  10.2 0.1 copy.21.gauge
  10.2 6.8 %collective-permute-done.above = bf16[2,3,128,256]{3,2,1,0:T(8,128)(2,1)S(1)} collective-permute-done((bf16[2,3,128,256]{3,2,1,0:T(8,128)(2,1)S(1)}, bf16[2,3,128,256]{3,2,1,0:T(8,128)(2,1)S(1)}, u32[]{:S(2)}, u32[]{:S(2)}) %collective-permute-start) | collective-permute-done | bytes 393248 | tf_op jit(solution)/shard_map/ppermute | solution.py:283
  17.0 0.0 copy-done
  17.0 5.1 %elementals.1 = bf16[4,2,128,128]{3,2,1,0:T(8,128)(2,1)S(1)} custom-call(s32[4]{0:T(128)S(1)} %copy-done.2, bf16[2,3,128,512]{3,2,1,0:T(8,128)(2,1)S(1)} %bitcast.45, bf16[2,3,128,256]{3,2,1,0:T(8,128)(2,1)S(1)} %collective-permute-done.above, f32[4,18,512]{2,1,0:T(8,128)S(1)} %copy.21.gauge), custom_call_target="tpu_custom_call" | custom-call | tf_op jit(solution)/shard_map/elementals/pallas_call | solution.py:288
  22.1 22.0 %exchange.1 = (f32[64,128]{1,0:T(8,128)S(1)}, bf16[32,64,128]{2,1,0:T(8,128)(2,1)S(1)}) custom-call(bf16[1024,128]{1,0:T(8,128)(2,1)S(1)} %bitcast.46), custom_call_target="tpu_custom_call" | custom-call | tf_op jit(solution)/shard_map/exchange/pallas_call | solution.py:302
  44.1 0.0 copy-start.3
  44.1 0.0 copy-done.1
  44.2 0.6 %copy-done.3 = s32[1,2]{1,0:T(1,128)S(1)} copy-done((s32[1,2]{1,0:T(1,128)S(1)}, s32[1,2]{1,0:T(1,128)}, u32[]{:S(2)}) %copy-start.3) | copy-done | bytes 32
  44.8 4.0 %correlate.1 = f32[1,4,2]{2,1,0:T(4,128)S(1)} custom-call(s32[1,2]{1,0:T(1,128)S(1)} %copy-done.3, bf16[2,4,2,128,128]{4,3,2,1,0:T(8,128)(2,1)S(1)} %bitcast.47, bf16[1,2,512,512]{3,2,1,0:T(8,128)(2,1)S(1)} %copy-done.1), custom_call_target="tpu_custom_call" | custom-call | tf_op jit(solution)/shard_map/correlate/pallas_call | solution.py:325
  48.8 0.6 %copy.22 = f32[1,4,2]{1,2,0:T(2,128)} copy(f32[1,4,2]{2,1,0:T(4,128)S(1)} %correlate.1) | data formatting | bytes 64
  49.4 0.6 %copy.48 = f32[64,128]{1,0:T(8,128)} copy(f32[64,128]{1,0:T(8,128)S(1)} %get-tuple-element.48) | data formatting | bytes 65536
  (13 shorter events, 0.2 us)
Async XLA Ops:
  0.6 8.0 %copy-start.4 = (bf16[1,3,2,3,3,512]{5,2,4,3,1,0:T(2,128)(2,1)S(1)}, bf16[1,3,2,3,3,512]{5,2,4,3,1,0:T(2,128)(2,1)}, u32[]{:S(2)}) copy-start(bf16[1,3,2,3,3,512]{5,2,4,3,1,0:T(2,128)(2,1)} %param.7) | copy-start | bytes 165892
  1.7 15.4 %collective-permute-start = (bf16[2,3,128,256]{3,2,1,0:T(8,128)(2,1)S(1)}, bf16[2,3,128,256]{3,2,1,0:T(8,128)(2,1)S(1)}, u32[]{:S(2)}, u32[]{:S(2)}) collective-permute-start(bf16[2,3,128,256]{3,2,1,0:T(8,128)(2,1)S(1)} %slice_bitcast_fusion), channel_id=1, source_target_pairs={{2,0},{3,1},{4,2},{5,3},{6,4},{7,5},{8,6},{9,7},{10,8},{11,9},{12,... | collective-permute-start | bytes 1179656 | tf_op jit(solution)/shard_map/ppermute | solution.py:283
  8.8 0.7 %copy-start.2 = (s32[4]{0:T(128)S(1)}, s32[4]{0:T(128)}, u32[]{:S(2)}) copy-start(s32[4]{0:T(128)} %codes.1) | copy-start | bytes 52
  8.8 0.7 %copy-start.5 = (s32[4,3]{1,0:T(4,128)S(1)}, s32[4,3]{1,0:T(4,128)}, u32[]{:S(2)}) copy-start(s32[4,3]{1,0:T(4,128)} %param.8) | copy-start | bytes 148
  8.9 8.2 %copy-start = (bf16[1,2,3,128,512]{4,3,2,1,0:T(8,128)(2,1)S(1)}, bf16[1,2,3,128,512]{4,3,2,1,0:T(8,128)(2,1)}, u32[]{:S(2)}) copy-start(bf16[1,2,3,128,512]{4,3,2,1,0:T(8,128)(2,1)} %param.6) | copy-start | bytes 2359300
  10.2 34.0 %copy-start.1 = (bf16[1,2,512,512]{3,2,1,0:T(8,128)(2,1)S(1)}, bf16[1,2,512,512]{3,2,1,0:T(8,128)(2,1)}, u32[]{:S(2)}) copy-start(bf16[1,2,512,512]{3,2,1,0:T(8,128)(2,1)} %tau.1) | copy-start | bytes 3145732
  44.1 0.7 %copy-start.3 = (s32[1,2]{1,0:T(1,128)S(1)}, s32[1,2]{1,0:T(1,128)}, u32[]{:S(2)}) copy-start(s32[1,2]{1,0:T(1,128)} %pairs.1) | copy-start | bytes 28
where the time goes:
time: 50.4 us; the launch traced here: 50 us
  Pallas kernels  31.1 us (62%)
  starting transfers between devices  6.98 us (14%)
  waiting for transfers between devices  6.79 us (13%)
  local copies, waits for them, and re-layouts  3.88 us (8%)
  between operations  0.83 us (2%)
    pallas_call x1, Pallas kernels, on_device(): pl.pallas_call(functools.partial(exchange_kernel, slab), out_shape=(jax.S...  22 us
    ppermute x1, starting transfers between devices, on_device(): above = lax.ppermute(eigvecs[0, ..., :plane], 'slab', route)  6.98 us
    ppermute x1, waiting for transfers between devices, on_device(): above = lax.ppermute(eigvecs[0, ..., :plane], 'slab', route)  6.79 us
    pallas_call x1, Pallas kernels, on_device(): pl.pallas_call(functools.partial(elementals_kernel, scale), out_shape=jax...  5.09 us
    pallas_call x1, Pallas kernels, on_device(): pl.pallas_call(correlate_kernel, grid=(pairs.shape[0],), out_shape=jax.Sh...  3.99 us
    unnamed x17, local copies, waits for them, and re-layouts  2.48 us
    squeeze x1, local copies, waits for them, and re-layouts, on_device(): above = lax.ppermute(eigvecs[0, ..., :plane], 'slab', route)  1.04 us
  transfers between devices with their start and end apart: 1, of which 1 were waited for; matrix products, arithmetic and copies ran while one was open for 2% of the time, Pallas kernels for 0%

commit v1 on v0

--- a/solution.py
+++ b/solution.py
@@ -18,9 +18,48 @@
 VMEM_LIMIT = 48 * 1024 * 1024
 
 
-def elementals_kernel(scale, codes, vecs, above, gauge, out, held, wave):
+def displace(gauge, field, left, wave, m, lanes_from, lanes_to, count, shift):
+    for start in range(lanes_from, lanes_to, 128):
+        lanes = pl.ds(start, 128)
+        near = pl.ds(start - shift, 128)
+        links = [gauge[m, pl.ds(k, 1), lanes] for k in range(18)]
+
+        def rows_step(r, carry, near=near, links=links):
+            row = pl.multiple_of(r * 16, 16)
+            fields = [
+                [field(b, pl.ds(part * count + row, 16), near) for part in range(2)]
+                for b in range(3)
+            ]
+            for c in range(3):
+                real = None
+                imag = None
+                for b in range(3):
+                    gr, gi = links[(c * 3 + b) * 2], links[(c * 3 + b) * 2 + 1]
+                    xr, xi = fields[b]
+                    tr = gr * xr - gi * xi
+                    ti = gr * xi + gi * xr
+                    real = tr if real is None else real + tr
+                    imag = ti if imag is None else imag + ti
+                wave[c, pl.ds(row, 16), near] = real.astype(jnp.bfloat16)
+                wave[c, pl.ds(count + row, 16), near] = imag.astype(jnp.bfloat16)
+            return carry
+
+        lax.fori_loop(0, count // 16, rows_step, 0, unroll=True)
+    whole = pl.ds(lanes_from - shift, lanes_to - lanes_from)
+    total = None
+    for c in range(3):
+        term = lax.dot_general(
+            left(c, whole),
+            wave[c, :, whole],
+            (((1,), (1,)), ((), ())),
+            preferred_element_type=jnp.float32,
+        )
+        total = term if total is None else total + term
+    return total
+
+
+def local_kernel(plane, codes, vecs, gauge, out, held, wave):
     count, sites = vecs.shape[2], vecs.shape[3]
-    plane = above.shape[3]
     lane = lax.broadcasted_iota(jnp.int32, (count, sites), 1)
     ends = {0: lane % LX == LX - 1, 1: (lane // LX) % LY == LY - 1}
 
@@ -42,54 +81,73 @@
             rows = pl.ds(part * count, count)
             held[3, c, rows, :] = vecs[part, c]
             held[2, c, rows, pl.ds(0, sites - plane)] = vecs[part, c, :, pl.ds(plane, sites - plane)]
-            held[2, c, rows, pl.ds(sites - plane, plane)] = above[part, c]
 
     for m in range(MOM):
-        code = codes[m]
-        axis = code // 2
-        forward = code % 2 == 0
+        axis = codes[m] // 2
+        forward = codes[m] % 2 == 0
         source = jnp.where(forward, axis, 3)
         left = jnp.where(forward, 3, axis)
-        for start in range(0, sites, 128):
-            lanes = pl.ds(start, 128)
-            links = [gauge[m, pl.ds(k, 1), lanes] for k in range(18)]
-
-            def rows_step(r, carry, lanes=lanes, links=links):
-                row = pl.multiple_of(r * 16, 16)
-                fields = [
-                    [
-                        held[source, b, pl.ds(part * count + row, 16), lanes].astype(jnp.float32)
-                        for part in range(2)
-                    ]
-                    for b in range(3)
-                ]
-                for c in range(3):
-                    real = None
-                    imag = None
-                    for b in range(3):
-                        gr, gi = links[(c * 3 + b) * 2], links[(c * 3 + b) * 2 + 1]
-                        xr, xi = fields[b]
-                        tr = gr * xr - gi * xi
-                        ti = gr * xi + gi * xr
-                        real = tr if real is None else real + tr
-                        imag = ti if imag is None else imag + ti
-                    wave[c, pl.ds(row, 16), lanes] = real.astype(jnp.bfloat16)
-                    wave[c, pl.ds(count + row, 16), lanes] = imag.astype(jnp.bfloat16)
-                return carry
-
-            lax.fori_loop(0, count // 16, rows_step, 0, unroll=True)
-        total = jnp.zeros((2 * count, 2 * count), jnp.float32)
+
+        def run(first, last, m=m, source=source, left=left):
+            return displace(
+                gauge,
+                lambda b, rows, lanes: held[source, b, rows, lanes].astype(jnp.float32),
+                lambda c, lanes: held[left, c, :, lanes],
+                wave,
+                m,
+                first,
+                last,
+                count,
+                0,
+            )
+
+        @pl.when(axis == 2)
+        def _(m=m, run=run):
+            out[m] = run(0, sites - plane)
+
+        @pl.when(axis != 2)
+        def _(m=m, run=run):
+            out[m] = run(0, sites)
+
+
+def border_kernel(scale, codes, vecs, above, gauge, inner, out, held, wave):
+    count, sites = vecs.shape[2], vecs.shape[3]
+    plane = above.shape[3]
+    for part in range(2):
         for c in range(3):
-            total = total + lax.dot_general(
-                held[left, c],
-                wave[c],
-                (((1,), (1,)), ((), ())),
-                preferred_element_type=jnp.float32,
-            )
+            rows = pl.ds(part * count, count)
+            held[0, c, rows, :] = vecs[part, c, :, pl.ds(sites - plane, plane)]
+            held[1, c, rows, :] = above[part, c]
+
+    def put(m, total):
         real = total[:count, :count] + total[count:, count:]
         imag = total[:count, count:] - total[count:, :count]
         out[m, 0] = (real * scale).astype(jnp.bfloat16)
         out[m, 1] = (imag * scale).astype(jnp.bfloat16)
+
+    for m in range(MOM):
+        axis = codes[m] // 2
+        forward = codes[m] % 2 == 0
+        source = jnp.where(forward, 1, 0)
+
+        @pl.when(axis == 2)
+        def _(m=m, source=source):
+            total = displace(
+                gauge,
+                lambda b, rows, lanes: held[source, b, rows, lanes].astype(jnp.float32),
+                lambda c, lanes: held[1 - source, c, :, lanes],
+                wave,
+                m,
+                sites - plane,
+                sites,
+                count,
+                sites - plane,
+            )
+            put(m, inner[m] + total)
+
+        @pl.when(axis != 2)
+        def _(m=m):
+            put(m, inner[m])
 
 
 def exchange_kernel(slab, part, mine, table, landed, held, send, arrive, send_far, send_near, got):
@@ -210,11 +268,15 @@
     table[...] = held[...]
 
 
-def correlate_kernel(pairs, phi, tau, out):
+def correlate_kernel(pairs, phi, tau, mine, out, rows_out):
     n = pl.program_id(0)
     first, second = pairs[n, 0], pairs[n, 1]
     count = phi.shape[-1]
     size = SPIN * count
+    rows_out[...] = mine[...]
+    row = lax.broadcasted_iota(jnp.int32, (2, MOM), 1)
+    part = lax.broadcasted_iota(jnp.int32, (2, MOM), 0)
+    values = jnp.zeros((2, MOM), jnp.float32)
     for m in range(MOM):
         fr, fi = phi[first, m, 0], phi[first, m, 1]
         sr, si = phi[second, m, 0], phi[second, m, 1]
@@ -242,8 +304,9 @@
                     real, imag = real + tr, imag + ti
                 else:
                     real, imag = real - tr, imag - ti
-        out[n, m, 0] = jnp.sum(real) / size
-        out[n, m, 1] = jnp.sum(imag) / size
+        both = jnp.where(part == 0, jnp.sum(real), jnp.sum(imag)) / size
+        values = jnp.where(row == m, both, values)
+    out[n] = values
 
 
 def phased_links(links, momenta, directions, zblock, depth):
@@ -285,18 +348,35 @@
     scale = 1.0 / math.sqrt(3.0 * site_count * ZBLK)
     vmem = pl.BlockSpec(memory_space=pltpu.VMEM)
     smem = pl.BlockSpec(memory_space=pltpu.SMEM)
-    part = pl.pallas_call(
-        functools.partial(elementals_kernel, scale),
-        out_shape=jax.ShapeDtypeStruct((MOM, 2, count, count), jnp.bfloat16),
-        in_specs=[smem, vmem, vmem, vmem],
+    inner = pl.pallas_call(
+        functools.partial(local_kernel, plane),
+        out_shape=jax.ShapeDtypeStruct((MOM, 2 * count, 2 * count), jnp.float32),
+        in_specs=[smem, vmem, vmem],
         out_specs=vmem,
         scratch_shapes=[
             pltpu.VMEM((4, 3, 2 * count, site_count), jnp.bfloat16),
             pltpu.VMEM((3, 2 * count, site_count), jnp.bfloat16),
         ],
         compiler_params=pltpu.CompilerParams(vmem_limit_bytes=VMEM_LIMIT),
-        name="elementals",
-    )(directions, eigvecs[0], above, gauge)
+        cost_estimate=pl.CostEstimate(
+            flops=MOM * 8 * count * count * 3 * site_count,
+            bytes_accessed=12 * count * site_count,
+            transcendentals=0,
+        ),
+        name="local",
+    )(directions, eigvecs[0], gauge)
+    part = pl.pallas_call(
+        functools.partial(border_kernel, scale),
+        out_shape=jax.ShapeDtypeStruct((MOM, 2, count, count), jnp.bfloat16),
+        in_specs=[smem, vmem, vmem, vmem, vmem],
+        out_specs=vmem,
+        scratch_shapes=[
+            pltpu.VMEM((2, 3, 2 * count, plane), jnp.bfloat16),
+            pltpu.VMEM((3, 2 * count, plane), jnp.bfloat16),
+        ],
+        compiler_params=pltpu.CompilerParams(vmem_limit_bytes=VMEM_LIMIT),
+        name="border",
+    )(directions, eigvecs[0], above, gauge, inner)
     part = part.reshape(MOM * 2 * count, count)
     share = part.shape[0] // ZBLK
     mine, table = pl.pallas_call(
@@ -322,20 +402,24 @@
         name="exchange",
     )(part)
     phi = table.reshape(groups, MOM, 2, count, count)
-    correlators = pl.pallas_call(
+    correlators, mine = pl.pallas_call(
         correlate_kernel,
         grid=(pairs.shape[0],),
-        out_shape=jax.ShapeDtypeStruct((pairs.shape[0], MOM, 2), jnp.float32),
+        out_shape=(
+            jax.ShapeDtypeStruct((pairs.shape[0], 2, MOM), jnp.float32),
+            jax.ShapeDtypeStruct((share, count), jnp.float32),
+        ),
         in_specs=[
             smem,
             vmem,
             pl.BlockSpec((1,) + perambulators.shape[1:], lambda n: (n, 0, 0, 0)),
+            vmem,
         ],
-        out_specs=smem,
+        out_specs=(vmem, vmem),
         compiler_params=pltpu.CompilerParams(vmem_limit_bytes=VMEM_LIMIT),
         name="correlate",
-    )(pairs, phi, perambulators)
-    return (mine, correlators)
+    )(jnp.clip(pairs, 0, groups - 1), phi, perambulators, mine)
+    return (mine, jnp.swapaxes(correlators, 1, 2))
 
 
 def solution(mesh):

time: 50.4 us -> 45.4 us (0.901)
  waiting for transfers between devices: 6.79 us -> 2.79 us
  local copies, waits for them, and re-layouts: 3.88 us -> 1.98 us
  Pallas kernels: 31.1 us -> 32.4 us
    ppermute x1, waiting for transfers between devices: 6.79 us -> 2.79 us  [on_device(): above = lax.ppermute(eigvecs[0, ..., :plane], 'slab', route)]
    unnamed x17 -> x15, local copies, waits for them, and re-layouts: 2.48 us -> 0.59 us
    pallas_call x2 -> x3, Pallas kernels: 9.08 us -> 10.4 us  [the longest x1 3.94 us: on_device(): pl.pallas_call(functools.partial(local_kernel, plane), out_shape=jax.Shap...]
  transfers between devices with their start and end apart: 1 -> 1, of which waited for: 1 -> 1; matrix products, arithmetic and copies ran while one was open for 2% -> 2% of each run, Pallas kernels for 0% -> 9%
where the time goes in v1:
time: 45.4 us; the launch traced here: 45.5 us
  Pallas kernels  32.4 us (71%)
  starting transfers between devices  6.98 us (15%)
  waiting for transfers between devices  2.79 us (6%)
  local copies, waits for them, and re-layouts  1.98 us (4%)
  between operations  0.85 us (2%)
  other arithmetic  0.51 us (1%)
    pallas_call x1, Pallas kernels, on_device(): pl.pallas_call(functools.partial(exchange_kernel, slab), out_shape=(jax.S...  22 us
    ppermute x1, starting transfers between devices, on_device(): above = lax.ppermute(eigvecs[0, ..., :plane], 'slab', route)  6.98 us
    pallas_call x1, Pallas kernels, on_device(): pl.pallas_call(functools.partial(local_kernel, plane), out_shape=jax.Shap...  3.94 us
    pallas_call x1, Pallas kernels, on_device(): pl.pallas_call(correlate_kernel, grid=(pairs.shape[0],), out_shape=(jax.S...  3.79 us
    ppermute x1, waiting for transfers between devices, on_device(): above = lax.ppermute(eigvecs[0, ..., :plane], 'slab', route)  2.79 us
    pallas_call x1, Pallas kernels, on_device(): pl.pallas_call(functools.partial(border_kernel, scale), out_shape=jax.Sha...  2.65 us
    squeeze x1, local copies, waits for them, and re-layouts, on_device(): above = lax.ppermute(eigvecs[0, ..., :plane], 'slab', route)  1.04 us
  transfers between devices with their start and end apart: 1, of which 1 were waited for; matrix products, arithmetic and copies ran while one was open for 2% of the time, Pallas kernels for 9%

profile of v1, /device:TPU:0, one launch (start us, length us, event | category | flops | bytes accessed | tf_op | source)
XLA Modules:
  0.0 45.5 jit_solution(5636074849323314035)
XLA Ops:
  0.6 0.0 copy-start.3
  0.6 1.0 %slice_bitcast_fusion = bf16[2,3,128,256]{3,2,1,0:T(8,128)(2,1)S(1)} fusion(bf16[1,2,3,128,512]{4,3,2,1,0:T(8,128)(2,1)} %param.6), kind=kLoop, calls=%fused_computation | loop fusion | bytes 786432 | tf_op jit(solution)/shard_map/squeeze | solution.py:346
  1.7 7.0 %collective-permute-start = (bf16[2,3,128,256]{3,2,1,0:T(8,128)(2,1)S(1)}, bf16[2,3,128,256]{3,2,1,0:T(8,128)(2,1)S(1)}, u32[]{:S(2)}, u32[]{:S(2)}) collective-permute-start(bf16[2,3,128,256]{3,2,1,0:T(8,128)(2,1)S(1)} %slice_bitcast_fusion), channel_id=1, source_target_pairs={{2,0},{3,1},{4,2},{5,3},{6,4},{7,5},{8,6},{9,7},{10,8},{11,9},{12,... | collective-permute-start | bytes 1179656 | tf_op jit(solution)/shard_map/ppermute | solution.py:346
  8.7 0.0 copy-done.3
  8.7 0.1 fusion.21
  8.8 0.0 copy-start.4
  8.8 0.0 copy-start.2
  8.9 0.0 copy-start
  9.0 0.5 %copy-done.4 = s32[4,3]{1,0:T(4,128)S(1)} copy-done((s32[4,3]{1,0:T(4,128)S(1)}, s32[4,3]{1,0:T(4,128)}, u32[]{:S(2)}) %copy-start.4) | copy-done | bytes 72
  9.5 0.2 slice_reduce_fusion.2
  9.7 0.0 copy-done.2
  9.7 0.2 fusion.20
  9.9 0.2 multiply_add_fusion
  10.2 0.1 copy.21.gauge
  10.2 0.0 copy-done
  10.2 0.0 copy-start.5
  10.3 3.9 %local.1.inner = f32[4,256,256]{2,1,0:T(8,128)S(1)} custom-call(s32[4]{0:T(128)S(1)} %copy-done.2, bf16[2,3,128,512]{3,2,1,0:T(8,128)(2,1)S(1)} %bitcast.46, f32[4,18,512]{2,1,0:T(8,128)S(1)} %copy.21.gauge), custom_call_target="tpu_custom_call" | custom-call | flops 805306368 | bytes 786432 | tf_op jit(solution)/shard_map/local/pallas_call | solution.py:351
  14.2 0.0 copy-done.5
  14.2 0.0 copy-start.1
  14.2 2.8 %collective-permute-done.above = bf16[2,3,128,256]{3,2,1,0:T(8,128)(2,1)S(1)} collective-permute-done((bf16[2,3,128,256]{3,2,1,0:T(8,128)(2,1)S(1)}, bf16[2,3,128,256]{3,2,1,0:T(8,128)(2,1)S(1)}, u32[]{:S(2)}, u32[]{:S(2)}) %collective-permute-start) | collective-permute-done | bytes 393248 | tf_op jit(solution)/shard_map/ppermute | solution.py:346
  17.0 2.7 %border.1 = bf16[4,2,128,128]{3,2,1,0:T(8,128)(2,1)S(1)} custom-call(s32[4]{0:T(128)S(1)} %copy-done.2, bf16[2,3,128,512]{3,2,1,0:T(8,128)(2,1)S(1)} %bitcast.47, bf16[2,3,128,256]{3,2,1,0:T(8,128)(2,1)S(1)} %collective-permute-done.above, f32[4,18,512]{2,1,0:T(8,128)S(1)} %copy.21.gauge, f32[4,256,256]{2,1,0:T(8,128)S(1)} %local.1.inner), custom_call_target="tpu_custom_call" | custom-call | tf_op jit(solution)/shard_map/border/pallas_call | solution.py:368
  19.7 22.0 %exchange.1 = (f32[64,128]{1,0:T(8,128)S(1)}, bf16[32,64,128]{2,1,0:T(8,128)(2,1)S(1)}) custom-call(bf16[1024,128]{1,0:T(8,128)(2,1)S(1)} %bitcast.48), custom_call_target="tpu_custom_call" | custom-call | tf_op jit(solution)/shard_map/exchange/pallas_call | solution.py:382
  41.7 0.0 copy-done.1
  41.7 3.8 %correlate.1 = (f32[1,2,4]{2,1,0:T(2,128)}, f32[64,128]{1,0:T(8,128)}) custom-call(s32[1,2]{1,0:T(1,128)S(1)} %broadcast_clamp_fusion.pairs, bf16[2,4,2,128,128]{4,3,2,1,0:T(8,128)(2,1)S(1)} %bitcast.49, bf16[1,2,512,512]{3,2,1,0:T(8,128)(2,1)S(1)} %copy-done.1, f32[64,128]{1,0:T(8,128)S(1)} %get-tuple-element.7.mine), custom_call_target="tpu_custom_call" | custom-call | tf_op jit(solution)/shard_map/correlate/pallas_call | solution.py:405
  (14 shorter events, 0.2 us)
Async XLA Ops:
  0.6 8.0 %copy-start.3 = (bf16[1,3,2,3,3,512]{5,2,4,3,1,0:T(2,128)(2,1)S(1)}, bf16[1,3,2,3,3,512]{5,2,4,3,1,0:T(2,128)(2,1)}, u32[]{:S(2)}) copy-start(bf16[1,3,2,3,3,512]{5,2,4,3,1,0:T(2,128)(2,1)} %param.7) | copy-start | bytes 165892
  1.7 15.4 %collective-permute-start = (bf16[2,3,128,256]{3,2,1,0:T(8,128)(2,1)S(1)}, bf16[2,3,128,256]{3,2,1,0:T(8,128)(2,1)S(1)}, u32[]{:S(2)}, u32[]{:S(2)}) collective-permute-start(bf16[2,3,128,256]{3,2,1,0:T(8,128)(2,1)S(1)} %slice_bitcast_fusion), channel_id=1, source_target_pairs={{2,0},{3,1},{4,2},{5,3},{6,4},{7,5},{8,6},{9,7},{10,8},{11,9},{12,... | collective-permute-start | bytes 1179656 | tf_op jit(solution)/shard_map/ppermute | solution.py:346
  8.8 0.7 %copy-start.4 = (s32[4,3]{1,0:T(4,128)S(1)}, s32[4,3]{1,0:T(4,128)}, u32[]{:S(2)}) copy-start(s32[4,3]{1,0:T(4,128)} %param.8) | copy-start | bytes 148
  8.8 0.9 %copy-start.2 = (s32[4]{0:T(128)S(1)}, s32[4]{0:T(128)}, u32[]{:S(2)}) copy-start(s32[4]{0:T(128)} %codes.3) | copy-start | bytes 52
  8.9 1.4 %copy-start = (bf16[1,2,3,128,512]{4,3,2,1,0:T(8,128)(2,1)S(1)}, bf16[1,2,3,128,512]{4,3,2,1,0:T(8,128)(2,1)}, u32[]{:S(2)}) copy-start(bf16[1,2,3,128,512]{4,3,2,1,0:T(8,128)(2,1)} %param.6) | copy-start | bytes 2359300
  10.2 4.0 %copy-start.5 = (s32[1,2]{1,0:T(1,128)S(1)}, s32[1,2]{1,0:T(1,128)}, u32[]{:S(2)}) copy-start(s32[1,2]{1,0:T(1,128)} %param.10) | copy-start | bytes 28
  14.2 27.5 %copy-start.1 = (bf16[1,2,512,512]{3,2,1,0:T(8,128)(2,1)S(1)}, bf16[1,2,512,512]{3,2,1,0:T(8,128)(2,1)}, u32[]{:S(2)}) copy-start(bf16[1,2,512,512]{3,2,1,0:T(8,128)(2,1)} %tau.1) | copy-start | bytes 3145732

commit v2 on v1

--- a/solution.py
+++ b/solution.py
@@ -27,7 +27,7 @@
         def rows_step(r, carry, near=near, links=links):
             row = pl.multiple_of(r * 16, 16)
             fields = [
-                [field(b, pl.ds(part * count + row, 16), near) for part in range(2)]
+                [field(part, b, row, near).astype(jnp.float32) for part in range(2)]
                 for b in range(3)
             ]
             for c in range(3):
@@ -91,7 +91,7 @@
         def run(first, last, m=m, source=source, left=left):
             return displace(
                 gauge,
-                lambda b, rows, lanes: held[source, b, rows, lanes].astype(jnp.float32),
+                lambda part, b, row, lanes: held[source, b, pl.ds(part * count + row, 16), lanes],
                 lambda c, lanes: held[left, c, :, lanes],
                 wave,
                 m,
@@ -110,14 +110,11 @@
             out[m] = run(0, sites)
 
 
-def border_kernel(scale, codes, vecs, above, gauge, inner, out, held, wave):
+def border_kernel(scale, codes, vecs, above, gauge, inner, out, wave):
     count, sites = vecs.shape[2], vecs.shape[3]
     plane = above.shape[3]
-    for part in range(2):
-        for c in range(3):
-            rows = pl.ds(part * count, count)
-            held[0, c, rows, :] = vecs[part, c, :, pl.ds(sites - plane, plane)]
-            held[1, c, rows, :] = above[part, c]
+    depth = sites - plane
+    top = vecs.at[:, :, :, pl.ds(depth, plane)]
 
     def put(m, total):
         real = total[:count, :count] + total[count:, count:]
@@ -125,25 +122,31 @@
         out[m, 0] = (real * scale).astype(jnp.bfloat16)
         out[m, 1] = (imag * scale).astype(jnp.bfloat16)
 
+    def step(m, moved, left):
+        total = displace(
+            gauge,
+            lambda part, b, row, lanes: moved[part, b, pl.ds(row, 16), lanes],
+            lambda c, lanes: jnp.concatenate([left[0, c, :, lanes], left[1, c, :, lanes]], axis=0),
+            wave,
+            m,
+            depth,
+            sites,
+            count,
+            depth,
+        )
+        put(m, inner[m] + total)
+
     for m in range(MOM):
         axis = codes[m] // 2
         forward = codes[m] % 2 == 0
-        source = jnp.where(forward, 1, 0)
-
-        @pl.when(axis == 2)
-        def _(m=m, source=source):
-            total = displace(
-                gauge,
-                lambda b, rows, lanes: held[source, b, rows, lanes].astype(jnp.float32),
-                lambda c, lanes: held[1 - source, c, :, lanes],
-                wave,
-                m,
-                sites - plane,
-                sites,
-                count,
-                sites - plane,
-            )
-            put(m, inner[m] + total)
+
+        @pl.when(jnp.logical_and(axis == 2, forward))
+        def _(m=m):
+            step(m, above, top)
+
+        @pl.when(jnp.logical_and(axis == 2, jnp.logical_not(forward)))
+        def _(m=m):
+            step(m, top, above)
 
         @pl.when(axis != 2)
         def _(m=m):
@@ -156,20 +159,26 @@
     me = lax.axis_index("slab")
     zblock, time = me // groups, me % groups
     own_time = me // ZBLK
-    chips = slab // 2
-    chip, core = me // 2, me % 2
-    partner = chip * 2 + (1 - core)
 
     barrier = pltpu.get_barrier_semaphore()
 
     def greet(j, carry):
-        pl.semaphore_signal(
-            barrier, inc=1, device_id={"slab": lax.rem(me + j, slab)}, device_id_type=MESH
-        )
-        return carry
-
-    lax.fori_loop(1, slab, greet, 0)
-    pl.semaphore_wait(barrier, slab - 1)
+        source = lax.rem(zblock + j, ZBLK) * groups + own_time
+
+        @pl.when(source != me)
+        def _():
+            pl.semaphore_signal(barrier, inc=1, device_id={"slab": source}, device_id_type=MESH)
+
+        return carry
+
+    lax.fori_loop(0, ZBLK, greet, 0)
+
+    def mate(j):
+        return zblock * groups + lax.rem(time + j, groups)
+
+    for j in range(1, groups):
+        pl.semaphore_signal(barrier, inc=1, device_id={"slab": mate(j)}, device_id_type=MESH)
+    pl.semaphore_wait(barrier, jnp.where(own_time == time, ZBLK - 1, ZBLK) + groups - 1)
 
     def piece(k):
         return pltpu.make_async_remote_copy(
@@ -187,7 +196,7 @@
             dst_ref=landed.at[z],
             send_sem=send.at[0],
             recv_sem=arrive.at[z],
-            device_id={"slab": partner},
+            device_id={"slab": lax.rem(me + 1, slab)},
             device_id_type=MESH,
         )
 
@@ -227,35 +236,57 @@
             device_id_type=MESH,
         )
 
-    block(me, partner, send_near.at[chip]).start()
-
     def send_far_block(j, carry):
-        target = lax.rem(chip + j, chips)
-        block(me, target * 2 + core, send_far.at[target]).start()
-        return carry
-
-    lax.fori_loop(1, chips, send_far_block, 0)
+        z = lax.rem(zblock + j, ZBLK)
+        target = z * groups + own_time
+
+        @pl.when(target != me)
+        def _():
+            block(me, target, send_far.at[z]).start()
+
+        return carry
+
+    lax.fori_loop(0, ZBLK, send_far_block, 0)
 
     def forward(j, carry):
-        origin = lax.rem(chip + chips - j, chips)
-        slot = origin * 2 + core
-        block(slot, partner, send_near.at[origin]).wait_recv()
-        block(slot, partner, send_near.at[origin]).start()
-        return carry
-
-    lax.fori_loop(1, chips, forward, 0)
-
-    def finish(c, carry):
-        block(c * 2 + 1 - core, partner, send_near.at[c]).wait_recv()
-        block(c * 2 + core, partner, send_near.at[c]).wait_send()
-
-        @pl.when(c != chip)
-        def _():
-            block(me, c * 2 + core, send_far.at[c]).wait_send()
-
-        return carry
-
-    lax.fori_loop(0, chips, finish, 0)
+        k = lax.rem(me + j, ZBLK)
+        slot = time * ZBLK + k
+
+        @pl.when(slot != me)
+        def _():
+            block(slot, mate(1), send_near.at[k]).wait_recv()
+
+        for i in range(1, groups):
+
+            @pl.when(slot != mate(i))
+            def _(i=i):
+                block(slot, mate(i), send_near.at[(i - 1) * ZBLK + k]).start()
+
+        return carry
+
+    lax.fori_loop(0, ZBLK, forward, 0)
+
+    def finish(k, carry):
+        for i in range(1, groups):
+            origin = lax.rem(time + groups - i, groups)
+
+            @pl.when(origin * ZBLK + k != me)
+            def _(origin=origin):
+                block(origin * ZBLK + k, mate(1), send_near.at[k]).wait_recv()
+
+        for i in range(1, groups):
+
+            @pl.when(time * ZBLK + k != mate(i))
+            def _(i=i):
+                block(time * ZBLK + k, mate(i), send_near.at[(i - 1) * ZBLK + k]).wait_send()
+
+        @pl.when(k * groups + own_time != me)
+        def _():
+            block(me, k * groups + own_time, send_far.at[k]).wait_send()
+
+        return carry
+
+    lax.fori_loop(0, ZBLK, finish, 0)
 
     def sent(k, carry):
         @pl.when(time * ZBLK + k != me)
@@ -371,7 +402,6 @@
         in_specs=[smem, vmem, vmem, vmem, vmem],
         out_specs=vmem,
         scratch_shapes=[
-            pltpu.VMEM((2, 3, 2 * count, plane), jnp.bfloat16),
             pltpu.VMEM((3, 2 * count, plane), jnp.bfloat16),
         ],
         compiler_params=pltpu.CompilerParams(vmem_limit_bytes=VMEM_LIMIT),
@@ -392,8 +422,8 @@
             pltpu.VMEM((slab, share, count), jnp.bfloat16),
             pltpu.SemaphoreType.DMA((ZBLK,)),
             pltpu.SemaphoreType.DMA((ZBLK,)),
-            pltpu.SemaphoreType.DMA((slab // 2,)),
-            pltpu.SemaphoreType.DMA((slab // 2,)),
+            pltpu.SemaphoreType.DMA((ZBLK,)),
+            pltpu.SemaphoreType.DMA(((groups - 1) * ZBLK,)),
             pltpu.SemaphoreType.DMA((slab,)),
         ],
         compiler_params=pltpu.CompilerParams(

time: 45.4 us -> 46.1 us (1.015)
  Pallas kernels: 32.4 us -> 33.1 us
    pallas_call x1, Pallas kernels: 22 us -> 22.5 us  [on_device(): pl.pallas_call(functools.partial(exchange_kernel, slab), out_shape=(jax.S...]
where the time goes in v2:
time: 46.1 us; the launch traced here: 46 us
  Pallas kernels  33.1 us (72%)
  starting transfers between devices  6.98 us (15%)
  waiting for transfers between devices  2.55 us (6%)
  local copies, waits for them, and re-layouts  1.98 us (4%)
  between operations  0.85 us (2%)
  other arithmetic  0.51 us (1%)
    pallas_call x1, Pallas kernels, on_device(): pl.pallas_call(functools.partial(exchange_kernel, slab), out_shape=(jax.S...  22.5 us
    ppermute x1, starting transfers between devices, on_device(): above = lax.ppermute(eigvecs[0, ..., :plane], 'slab', route)  6.98 us
    pallas_call x1, Pallas kernels, on_device(): pl.pallas_call(functools.partial(local_kernel, plane), out_shape=jax.Shap...  4.19 us
    pallas_call x1, Pallas kernels, on_device(): pl.pallas_call(correlate_kernel, grid=(pairs.shape[0],), out_shape=(jax.S...  3.8 us
    pallas_call x1, Pallas kernels, on_device(): pl.pallas_call(functools.partial(border_kernel, scale), out_shape=jax.Sha...  2.64 us
    ppermute x1, waiting for transfers between devices, on_device(): above = lax.ppermute(eigvecs[0, ..., :plane], 'slab', route)  2.55 us
    squeeze x1, local copies, waits for them, and re-layouts, on_device(): above = lax.ppermute(eigvecs[0, ..., :plane], 'slab', route)  1.04 us
  transfers between devices with their start and end apart: 1, of which 1 were waited for; matrix products, arithmetic and copies ran while one was open for 2% of the time, Pallas kernels for 9%

profile of v2, /device:TPU:0, one launch (start us, length us, event | category | flops | bytes accessed | tf_op | source)
XLA Modules:
  0.0 46.0 jit_solution(16925962733404008867)
XLA Ops:
  0.6 0.0 copy-start.3
  0.6 1.0 %slice_bitcast_fusion = bf16[2,3,128,256]{3,2,1,0:T(8,128)(2,1)S(1)} fusion(bf16[1,2,3,128,512]{4,3,2,1,0:T(8,128)(2,1)} %param.6), kind=kLoop, calls=%fused_computation | loop fusion | bytes 786432 | tf_op jit(solution)/shard_map/squeeze | solution.py:377
  1.7 7.0 %collective-permute-start = (bf16[2,3,128,256]{3,2,1,0:T(8,128)(2,1)S(1)}, bf16[2,3,128,256]{3,2,1,0:T(8,128)(2,1)S(1)}, u32[]{:S(2)}, u32[]{:S(2)}) collective-permute-start(bf16[2,3,128,256]{3,2,1,0:T(8,128)(2,1)S(1)} %slice_bitcast_fusion), channel_id=1, source_target_pairs={{2,0},{3,1},{4,2},{5,3},{6,4},{7,5},{8,6},{9,7},{10,8},{11,9},{12,... | collective-permute-start | bytes 1179656 | tf_op jit(solution)/shard_map/ppermute | solution.py:377
  8.7 0.0 copy-done.3
  8.7 0.1 fusion.21
  8.8 0.0 copy-start.4
  8.8 0.0 copy-start.2
  8.9 0.0 copy-start
  9.0 0.5 %copy-done.4 = s32[4,3]{1,0:T(4,128)S(1)} copy-done((s32[4,3]{1,0:T(4,128)S(1)}, s32[4,3]{1,0:T(4,128)}, u32[]{:S(2)}) %copy-start.4) | copy-done | bytes 72
  9.5 0.2 slice_reduce_fusion.2
  9.7 0.0 copy-done.2
  9.7 0.2 fusion.20
  9.9 0.2 multiply_add_fusion
  10.2 0.1 copy.21.gauge
  10.2 0.0 copy-done
  10.2 0.0 copy-start.5
  10.3 4.2 %local.1.inner = f32[4,256,256]{2,1,0:T(8,128)S(1)} custom-call(s32[4]{0:T(128)S(1)} %copy-done.2, bf16[2,3,128,512]{3,2,1,0:T(8,128)(2,1)S(1)} %bitcast.46, f32[4,18,512]{2,1,0:T(8,128)S(1)} %copy.21.gauge), custom_call_target="tpu_custom_call" | custom-call | flops 805306368 | bytes 786432 | tf_op jit(solution)/shard_map/local/pallas_call | solution.py:382
  14.5 0.0 copy-done.5
  14.5 0.0 copy-start.1
  14.5 2.5 %collective-permute-done.above = bf16[2,3,128,256]{3,2,1,0:T(8,128)(2,1)S(1)} collective-permute-done((bf16[2,3,128,256]{3,2,1,0:T(8,128)(2,1)S(1)}, bf16[2,3,128,256]{3,2,1,0:T(8,128)(2,1)S(1)}, u32[]{:S(2)}, u32[]{:S(2)}) %collective-permute-start) | collective-permute-done | bytes 393248 | tf_op jit(solution)/shard_map/ppermute | solution.py:377
  17.0 2.6 %border.1 = bf16[4,2,128,128]{3,2,1,0:T(8,128)(2,1)S(1)} custom-call(s32[4]{0:T(128)S(1)} %copy-done.2, bf16[2,3,128,512]{3,2,1,0:T(8,128)(2,1)S(1)} %bitcast.47, bf16[2,3,128,256]{3,2,1,0:T(8,128)(2,1)S(1)} %collective-permute-done.above, f32[4,18,512]{2,1,0:T(8,128)S(1)} %copy.21.gauge, f32[4,256,256]{2,1,0:T(8,128)S(1)} %local.1.inner), custom_call_target="tpu_custom_call" | custom-call | tf_op jit(solution)/shard_map/border/pallas_call | solution.py:399
  19.7 22.5 %exchange.1 = (f32[64,128]{1,0:T(8,128)S(1)}, bf16[32,64,128]{2,1,0:T(8,128)(2,1)S(1)}) custom-call(bf16[1024,128]{1,0:T(8,128)(2,1)S(1)} %bitcast.48), custom_call_target="tpu_custom_call" | custom-call | tf_op jit(solution)/shard_map/exchange/pallas_call | solution.py:412
  42.2 0.0 copy-done.1
  42.2 3.8 %correlate.1 = (f32[1,2,4]{2,1,0:T(2,128)}, f32[64,128]{1,0:T(8,128)}) custom-call(s32[1,2]{1,0:T(1,128)S(1)} %broadcast_clamp_fusion.pairs, bf16[2,4,2,128,128]{4,3,2,1,0:T(8,128)(2,1)S(1)} %bitcast.49, bf16[1,2,512,512]{3,2,1,0:T(8,128)(2,1)S(1)} %copy-done.1, f32[64,128]{1,0:T(8,128)S(1)} %get-tuple-element.7.mine), custom_call_target="tpu_custom_call" | custom-call | tf_op jit(solution)/shard_map/correlate/pallas_call | solution.py:435
  (14 shorter events, 0.2 us)
Async XLA Ops:
  0.6 8.0 %copy-start.3 = (bf16[1,3,2,3,3,512]{5,2,4,3,1,0:T(2,128)(2,1)S(1)}, bf16[1,3,2,3,3,512]{5,2,4,3,1,0:T(2,128)(2,1)}, u32[]{:S(2)}) copy-start(bf16[1,3,2,3,3,512]{5,2,4,3,1,0:T(2,128)(2,1)} %param.7) | copy-start | bytes 165892
  1.7 15.4 %collective-permute-start = (bf16[2,3,128,256]{3,2,1,0:T(8,128)(2,1)S(1)}, bf16[2,3,128,256]{3,2,1,0:T(8,128)(2,1)S(1)}, u32[]{:S(2)}, u32[]{:S(2)}) collective-permute-start(bf16[2,3,128,256]{3,2,1,0:T(8,128)(2,1)S(1)} %slice_bitcast_fusion), channel_id=1, source_target_pairs={{2,0},{3,1},{4,2},{5,3},{6,4},{7,5},{8,6},{9,7},{10,8},{11,9},{12,... | collective-permute-start | bytes 1179656 | tf_op jit(solution)/shard_map/ppermute | solution.py:377
  8.8 0.7 %copy-start.4 = (s32[4,3]{1,0:T(4,128)S(1)}, s32[4,3]{1,0:T(4,128)}, u32[]{:S(2)}) copy-start(s32[4,3]{1,0:T(4,128)} %param.8) | copy-start | bytes 148
  8.8 0.9 %copy-start.2 = (s32[4]{0:T(128)S(1)}, s32[4]{0:T(128)}, u32[]{:S(2)}) copy-start(s32[4]{0:T(128)} %codes.3) | copy-start | bytes 52
  8.9 1.4 %copy-start = (bf16[1,2,3,128,512]{4,3,2,1,0:T(8,128)(2,1)S(1)}, bf16[1,2,3,128,512]{4,3,2,1,0:T(8,128)(2,1)}, u32[]{:S(2)}) copy-start(bf16[1,2,3,128,512]{4,3,2,1,0:T(8,128)(2,1)} %param.6) | copy-start | bytes 2359300
  10.2 4.2 %copy-start.5 = (s32[1,2]{1,0:T(1,128)S(1)}, s32[1,2]{1,0:T(1,128)}, u32[]{:S(2)}) copy-start(s32[1,2]{1,0:T(1,128)} %param.10) | copy-start | bytes 28
  14.5 27.7 %copy-start.1 = (bf16[1,2,512,512]{3,2,1,0:T(8,128)(2,1)S(1)}, bf16[1,2,512,512]{3,2,1,0:T(8,128)(2,1)}, u32[]{:S(2)}) copy-start(bf16[1,2,512,512]{3,2,1,0:T(8,128)(2,1)} %tau.1) | copy-start | bytes 3145732
